TPU v7x, 256 devices: a whole 4x4x8 slice. The times are simulated.
256 devices in a mesh: dp: 16 (over z_hi, x), expert: 16 (over z_lo, y, core).
Axes of the slice: x: 4, y: 4, z: 8 (z_hi: 4, z_lo: 2; z = z_hi * 2 + z_lo), core: 2. Of those that a mesh axis runs over, the one named last changes fastest.
Arguments:
- tokens: bfloat16 [512, 256, 1280], P(('dp', 'expert')), may hold values from -6 to 6
- logits: float32 [512, 256, 32], P(('dp', 'expert')), may hold values from -20 to 320
- out_grad: bfloat16 [512, 256, 1280], P(('dp', 'expert')), may hold values from -6 to 6
- w_in: bfloat16 [32, 5120, 1280], P('expert', 'dp'), may hold values from -0.15625 to 0.15625
- w_out: bfloat16 [32, 5120, 1280], P('expert', 'dp'), may hold values from -0.078125 to 0.078125
Outputs:
- token_grad: bfloat16 [512, 256, 1280], P(('dp', 'expert'))
- logit_grad: float32 [512, 256, 32], P(('dp', 'expert'))
- w_in_grad: bfloat16 [32, 5120, 1280], P('expert', 'dp')
- w_out_grad: bfloat16 [32, 5120, 1280], P('expert', 'dp')
All inputs are finite; a program needn't handle non-finite values.
Results may differ from a plain program's by a relative error of at most 0.008.
Values may be sent and summed in bfloat16 or wider, within the bound.
A program may use at most 128 MiB of HBM per device.

v0:
```python
import jax
import jax.numpy as jnp
from jax import lax
from jax.experimental import pallas as pl
from jax.experimental.pallas import tpu as pltpu
from jax.sharding import PartitionSpec as P

RING = 4
TILE = 128
SPLIT = 1024
MESH = pl.DeviceIdType.MESH
BF16 = jnp.bfloat16
F32 = jnp.float32


def normal_cdf(values):
    return 0.5 * (1.0 + lax.erf(values * 0.7071067811865476))


def soft_weights(values, over_dim):
    highest = jnp.max(values, axis=over_dim, keepdims=True)
    raised = jnp.exp(values - highest)
    return raised / jnp.sum(raised, axis=over_dim, keepdims=True)


def shift(at, by, size):
    return lax.rem(at + (by + size), size)


def iota(shape, dim):
    return lax.broadcasted_iota(jnp.int32, shape, dim)


def zero_one(mask):
    return mask.astype(F32).astype(BF16)


def tiled(block, group):
    packed, features = block.shape
    pieces = [
        block[:, at * TILE:(at + 1) * TILE].reshape(group, 1, packed // group, TILE)
        for at in range(features // TILE)
    ]
    if len(pieces) % 2:
        pieces.append(jnp.zeros_like(pieces[0]))
    block = jnp.concatenate(pieces, axis=1)
    return block.reshape(group, len(pieces) * (packed // group), TILE).astype(BF16)


def untiled(block, features):
    group, high, _ = block.shape
    block = block.astype(F32).reshape(group, high // 8, 8, TILE)
    return jnp.concatenate(
        [block[:, at].reshape(group * 8, TILE) for at in range(features // TILE)], axis=1
    ).astype(BF16)


def picker(packed, half, by_member):
    shape = (packed // 2, packed)
    row, column = iota(shape, 0), iota(shape, 1)
    first, source, second = row // (packed // 4), (row % (packed // 4)) // 2, row % 2
    image, member = (second, first) if by_member else (first, second)
    return zero_one(column == ((source * 2 + half) * 2 + image) * 2 + member)


def unpack(block, depth, by_member):
    block = untiled(block, depth // 2)
    return jnp.concatenate(
        [jnp.dot(picker(block.shape[0], half, by_member), block, preferred_element_type=F32)
         for half in range(2)],
        axis=1,
    ).astype(BF16)


def pack(block):
    rows, depth = block.shape
    return sum(
        lax.dot_general(picker(2 * rows, half, True), block[:, half * depth // 2:(half + 1) * depth // 2],
                        (((0,), (0,)), ((), ())), preferred_element_type=F32)
        for half in range(2)
    )


ORDER = (
    ("make", 0), ("make", 1), ("own", 0), ("g1", 0, 0), ("s1", 0, 0, 0), ("g1", 0, 1), ("own", 1), ("g1", 1, 1),
    ("weights",), ("s1", 1, 0, 0), ("g1", 1, 0), ("s2t", 0, 0, 0, 0), ("s2t", 0, 0, 0, 1), ("g2t", 0, 1, 0),
    ("g2t", 1, 1, 1), ("g2t", 0, 1, 1), ("g2t", 1, 1, 0), ("s2t", 1, 0, 0, 0), ("s2t", 1, 0, 0, 1),
    ("g2t", 0, 0, 1), ("g2t", 0, 0, 0), ("s1", 0, 0, 2), ("g", 0, 0, 0), ("s1", 0, 0, 1), ("s1", 0, 1, 2),
    ("g", 1, 0, 0), ("s1", 0, 1, 1), ("s1", 0, 1, 0), ("s2t", 0, 0, 2, 0), ("s2t", 0, 0, 2, 1), ("s1", 0, 0, 3),
    ("s1", 0, 1, 3), ("s2t", 0, 1, 2, 0), ("g2t", 1, 0, 1), ("g2t", 1, 0, 0), ("s2t", 0, 0, 1, 0),
    ("s2t", 0, 0, 1, 1), ("g", 0, 0, 2), ("s1", 1, 0, 2), ("s2t", 0, 1, 1, 1), ("s2t", 0, 1, 1, 0),
    ("s2t", 0, 1, 0, 1), ("s2t", 0, 1, 0, 0), ("s2t", 0, 1, 3, 1), ("s2t", 0, 1, 3, 0), ("s2t", 0, 0, 3, 0),
    ("s2t", 0, 0, 3, 1), ("s1", 1, 1, 2), ("g", 0, 0, 1), ("s2t", 0, 1, 2, 1), ("s1", 1, 0, 1), ("s1", 1, 1, 3),
    ("g", 0, 1, 1), ("s1", 1, 1, 1), ("g", 0, 1, 0), ("s2t", 1, 0, 2, 0), ("s2t", 1, 0, 2, 1), ("g", 0, 1, 3),
    ("s1", 1, 1, 0), ("g", 0, 0, 3), ("s1", 1, 0, 3), ("g", 0, 1, 2), ("part", 0, 3, 1), ("part", 0, 3, 0),
    ("part", 0, 0, 1), ("part", 0, 1, 1), ("s2t", 1, 0, 1, 0), ("s2t", 1, 0, 1, 1), ("part", 0, 2, 0),
    ("s2t", 1, 1, 1, 1), ("s2t", 1, 1, 1, 0), ("s2t", 1, 1, 3, 1), ("s2t", 1, 1, 3, 0), ("s2t", 1, 1, 2, 0),
    ("r1", 0, 0, 3), ("part", 0, 0, 0), ("s2t", 1, 1, 0, 1), ("s2t", 1, 1, 2, 1), ("s2t", 1, 1, 0, 0),
    ("part", 0, 2, 1), ("r1", 0, 0, 2), ("part", 0, 1, 0), ("r1", 0, 1, 0), ("s2t", 1, 0, 3, 1),
    ("r1", 0, 0, 1), ("r1", 0, 1, 1), ("g", 1, 1, 1), ("r1", 0, 1, 3), ("r1", 0, 1, 2), ("g", 1, 1, 3),
    ("g", 1, 0, 2), ("g", 1, 0, 1), ("s2t", 1, 0, 3, 0), ("g", 1, 1, 2), ("g", 1, 1, 0), ("part", 1, 1, 1),
    ("part", 1, 2, 0), ("r2t", 0, 0, 3, 0), ("r2t", 0, 1, 1, 1), ("r2t", 0, 0, 3, 1), ("r2t", 0, 1, 0, 0),
    ("r2t", 0, 1, 1, 0), ("r2t", 0, 1, 0, 1), ("part", 1, 2, 1), ("r2t", 0, 1, 3, 1), ("part", 1, 0, 0),
    ("r2t", 0, 1, 2, 0), ("part", 1, 0, 1), ("r2t", 0, 0, 2, 0), ("r2t", 0, 0, 2, 1), ("r2t", 0, 1, 3, 0),
    ("r2t", 0, 1, 2, 1), ("part", 1, 1, 0), ("g", 1, 0, 3), ("weight", 1, 0), ("part", 1, 3, 1),
    ("part", 1, 3, 0), ("r1", 1, 0, 3), ("r", 0, 1, 1), ("r1", 1, 1, 0), ("r1", 1, 1, 1), ("weight", 0, 0),
    ("r2t", 0, 0, 1, 1), ("r2t", 0, 0, 1, 0), ("r", 0, 0, 3), ("t1", 0, 0), ("weight", 0, 1), ("store", 0),
    ("r", 0, 1, 2), ("r", 0, 1, 0), ("weight", 1, 1), ("r", 0, 1, 3), ("store", 1), ("r2t", 1, 1, 0, 1),
    ("r1", 1, 1, 3), ("r2t", 1, 1, 0, 0), ("r", 0, 0, 2), ("r1", 1, 0, 1), ("r2t", 1, 1, 1, 1), ("r1", 1, 1, 2),
    ("r2t", 1, 0, 3, 0), ("r2t", 1, 0, 3, 1), ("r2t", 1, 1, 1, 0), ("t2t", 0, 0, 0), ("r", 0, 0, 1),
    ("r1", 1, 0, 2), ("t2t", 0, 0, 1), ("r", 1, 1, 0), ("r2t", 1, 0, 1, 0), ("r2t", 1, 0, 1, 1), ("r", 1, 1, 1),
    ("r", 1, 0, 3), ("r1", 0, 0, 0), ("t1", 1, 0), ("r2t", 1, 0, 2, 0), ("r2t", 1, 0, 2, 1),
    ("r2t", 1, 1, 3, 1), ("r2t", 1, 1, 3, 0), ("r", 1, 0, 1), ("t1", 0, 1), ("r2t", 1, 1, 2, 1),
    ("r1", 1, 0, 0), ("r2t", 1, 1, 2, 0), ("r2t", 0, 0, 0, 0), ("r2t", 0, 0, 0, 1), ("t2t", 1, 0, 1),
    ("r", 1, 0, 2), ("t2t", 1, 0, 0), ("r", 1, 1, 3), ("t2t", 0, 1, 0), ("t1", 1, 1), ("t2t", 0, 1, 1),
    ("r2t", 1, 0, 0, 0), ("r2t", 1, 0, 0, 1), ("r", 1, 1, 2), ("r", 0, 0, 0), ("t", 0, 0), ("t2t", 1, 1, 1),
    ("t2t", 1, 1, 0), ("t", 0, 1), ("back", 0), ("r", 1, 0, 0), ("t", 1, 0), ("t", 1, 1), ("back", 1),
    ("finish", 0), ("finish", 1),
)


def kernel(
    tokens, logits_ref, out_grad, w_in_ref, w_out_ref,
    slot_in_grad_ref, from_combine_ref, w_in_grad_ref, w_out_grad_ref,
    combine, outbox, inbox, back_outbox, back_inbox,
    rows, part, half_a, full_a, half_b, full_b, last_half, last_full, total,
    w_in, w_out, slope, hidden, pre_grad, w_in_grad, w_out_grad,
    load_sem, store_sem, swap_send, swap_recv, send_sem, recv_sem,
):
    members, count, depth = rows.shape[3:]
    images, slots, length = combine.shape
    group = slots // members
    packed = group * 2 * images * members
    me = lax.axis_index("dp")
    mine = lax.axis_index("expert")
    at = {"z": me // RING, "x": lax.rem(me, RING)}
    to = {axis: (shift(at[axis], 1, RING), shift(at[axis], -1, RING)) for axis in "zx"}
    come = {axis: (to[axis][1], to[axis][0]) for axis in "zx"}
    across = {axis: shift(at[axis], 2, RING) for axis in "zx"}
    device = {
        "z": tuple(z * RING + at["x"] for z in to["z"]),
        "x": tuple(at["z"] * RING + x for x in to["x"]),
    }
    chunk = {axis: (at[axis], come[axis][0], come[axis][1], across[axis]) for axis in "zx"}
    halves = (
        ("z", "x", pl.ds(0, SPLIT)),
        ("x", "z", pl.ds(SPLIT, depth - SPLIT)),
    )
    width = (SPLIT, depth - SPLIT)
    half_buf, full_buf = (half_a, half_b), (full_a, full_b)

    def partner(by):
        return lax.rem(mine + by, group)

    barrier = pltpu.get_barrier_semaphore()
    for axis in "zx":
        for there in device[axis]:
            pl.semaphore_signal(barrier, inc=1, device_id={"dp": there}, device_id_type=MESH)

    def greet(by, carry):
        pl.semaphore_signal(barrier, inc=1, device_id={"expert": partner(by)}, device_id_type=MESH)
        return carry

    lax.fori_loop(1, group, greet, 0)

    loads = [
        pltpu.make_async_copy(source, target, load_sem.at[i])
        for i, (source, target) in enumerate(
            ((w_in_ref, w_in), (w_out_ref, w_out))
        )
    ]
    for load in loads:
        load.start()

    def swap_copy(kind, way, by, box, inbound):
        return pltpu.make_async_remote_copy(
            src_ref=box.at[kind, partner(by)], dst_ref=inbound.at[kind, mine],
            send_sem=swap_send.at[way, kind, by], recv_sem=swap_recv.at[way, kind, by],
            device_id={"expert": partner(by)}, device_id_type=MESH,
        )

    def swap_start(kind, way, box, inbound):
        def one(by, carry):
            swap_copy(kind, way, by, box, inbound).start()
            return carry

        lax.fori_loop(1, group, one, 0)
        inbound[kind, mine] = box[kind, mine]

    def swap_arrived(kind, way, box, inbound):
        def one(by, carry):
            swap_copy(kind, way, by, box, inbound).wait_recv()
            return carry

        lax.fori_loop(1, group, one, 0)

    def make_slots(kind):
        source = (tokens, out_grad)[kind]
        left = []
        for image in range(images):
            soft = soft_weights(logits_ref[image], 1 - kind)
            if kind == 1:
                combine[image] = soft
            row, slot = iota((packed, slots), 0), iota((packed, slots), 1)
            spread = zero_one((slot == (row // 8) * 2 + row % 2) & ((row // 2) % 2 == image))
            left.append(jnp.dot(spread, soft.astype(BF16), preferred_element_type=F32).astype(BF16))
        slot = jnp.dot(jnp.concatenate(left, axis=1), source[...].reshape(images * length, depth),
                       preferred_element_type=F32)
        first = (iota((packed, depth // 2), 0) // 4) % 2 == 0
        outbox[kind] = tiled(jnp.where(first, slot[:, :depth // 2], slot[:, depth // 2:]), group)

    def own_rows(kind):
        swap_arrived(kind, 0, outbox, inbox)
        rows[kind, at["z"], at["x"]] = unpack(inbox[kind], depth, True).reshape(members, count, depth)

    def send_back(kind):
        back_outbox[kind] = tiled(pack(total[kind].reshape(members * count, depth)), group)
        swap_start(kind, 1, back_outbox, back_inbox)

    def finish(kind):
        swap_arrived(kind, 1, back_outbox, back_inbox)
        back = unpack(back_inbox[kind], depth, False)
        if kind == 1:
            slot_in_grad_ref[...] = back
            return
        for image in range(images):
            grad = lax.dot_general(back[image * slots:(image + 1) * slots], out_grad[image],
                                   (((1,), (1,)), ((), ())), preferred_element_type=F32)
            soft = combine[image]
            from_combine_ref[image] = soft * (grad - jnp.sum(soft * grad, axis=0, keepdims=True))

    sent = []
    flying = {}

    def send(key, source, target, there):
        copy = pltpu.make_async_remote_copy(
            src_ref=source, dst_ref=target,
            send_sem=send_sem.at[len(sent)], recv_sem=recv_sem.at[len(sent)],
            device_id={"dp": there}, device_id_type=MESH,
        )
        copy.start()
        sent.append(copy)
        flying[key] = copy

    def arrived(key):
        flying.pop(key).wait_recv()

    def block(ref, kind, p, first, second, member=None):
        z, x = (first, second) if halves[p][0] == "z" else (second, first)
        return ref.at[kind, z, x, slice(None) if member is None else member, :, halves[p][2]]

    tasks = {}

    def gather(kind, p):
        one, two, _ = halves[p]

        def along_one():
            mine_here = block(rows, kind, p, at[one], at[two])
            for way in range(2):
                send(("g1", kind, p, way), mine_here, mine_here, device[one][way])

        tasks["g1", kind, p] = along_one
        for way in range(2):
            def on_one(way=way):
                arrived(("g1", kind, p, way))
                piece = block(rows, kind, p, come[one][way], at[two], way)
                send(("g2", kind, p, way), piece, piece, device[one][way])

            tasks["g2t", kind, p, way] = on_one

        for c in range(RING):
            def along_two(c=c):
                if c == 3:
                    for way in range(2):
                        arrived(("g2", kind, p, way))
                here = block(rows, kind, p, chunk[one][c], at[two])
                for way in range(2):
                    send(("s1", kind, p, c, way), here, here, device[two][way])

            tasks["s1", kind, p, c] = along_two
            for way in range(2):
                def on_two(c=c, way=way):
                    arrived(("s1", kind, p, c, way))
                    piece = block(rows, kind, p, chunk[one][c], come[two][way], way)
                    send(("s2", kind, p, c, way), piece, piece, device[two][way])

                tasks["s2t", kind, p, c, way] = on_two

            def gathered(c=c):
                for way in range(2):
                    arrived(("s2", kind, p, c, way))

            tasks["g", kind, p, c] = gathered

    def plus(*refs):
        value = refs[0][...].astype(F32)
        for ref in refs[1:]:
            value = value + ref[...].astype(F32)
        return value.astype(BF16)

    def reduce(kind, p):
        one, two, features = halves[p]
        half_in, full_in = half_buf[p], full_buf[p]
        for c in range(RING):
            def away(c=c):
                for way in range(2):
                    send(("r1", kind, p, c, way),
                         block(part, kind, p, chunk[one][c], across[two], way),
                         half_in.at[kind, c, way], device[two][way])

            tasks["r1", kind, p, c] = away
            for way in range(2):
                def add_on(c=c, way=way):
                    arrived(("r1", kind, p, c, way))
                    piece = block(part, kind, p, chunk[one][c], to[two][way], way)
                    piece[...] = plus(piece, half_in.at[kind, c, way])
                    send(("r2", kind, p, c, way), block(part, kind, p, chunk[one][c], to[two][way]),
                         full_in.at[kind, c, way], device[two][way])

                tasks["r2t", kind, p, c, way] = add_on

            def summed(c=c):
                for way in range(2):
                    arrived(("r2", kind, p, c, way))
                here = block(part, kind, p, chunk[one][c], at[two])
                here[...] = plus(here, full_in.at[kind, c, 0], full_in.at[kind, c, 1])

            tasks["r", kind, p, c] = summed

        last_h = last_half.at[kind, :, :, features]
        last_f = last_full.at[kind, :, :, :, features]

        def last_away():
            for way in range(2):
                send(("t1", kind, p, way), block(part, kind, p, across[one], at[two], way),
                     last_h.at[way], device[one][way])

        tasks["t1", kind, p] = last_away
        for way in range(2):
            def last_on(way=way):
                arrived(("t1", kind, p, way))
                piece = block(part, kind, p, to[one][way], at[two], way)
                piece[...] = plus(piece, last_h.at[way])
                send(("t2", kind, p, way), block(part, kind, p, to[one][way], at[two]),
                     last_f.at[way], device[one][way])

            tasks["t2t", kind, p, way] = last_on

        def last_sum():
            for way in range(2):
                arrived(("t2", kind, p, way))
            total[kind, :, :, features] = plus(
                block(part, kind, p, at[one], at[two]), last_f.at[0], last_f.at[1])

        tasks["t", kind, p] = last_sum

    def chunk_rows(kind, c, e):
        return rows[kind, chunk["z"][c], :, e].reshape(RING * count, depth)

    def place(c):
        return pl.ds(pl.multiple_of(chunk["z"][c] * (RING * count), RING * count), RING * count)

    def forward(c, e):
        pre = lax.dot_general(chunk_rows(0, c, e), w_in[e], (((1,), (1,)), ((), ())),
                              preferred_element_type=F32)
        cdf = normal_cdf(pre)
        act = (pre * cdf).astype(BF16)
        slope[e, place(c)] = cdf + pre * jnp.exp(-0.5 * pre * pre) * 0.3989422804014327
        hidden[e, place(c)] = act
        out = jnp.dot(act, w_out[e], preferred_element_type=F32)
        part[0, chunk["z"][c], :, e] = out.astype(BF16).reshape(RING, count, depth)

    def backward(c, e):
        grad = lax.dot_general(chunk_rows(1, c, e), w_out[e], (((1,), (1,)), ((), ())),
                               preferred_element_type=F32)
        grad = (grad * slope[e, place(c)]).astype(BF16)
        pre_grad[e, place(c)] = grad
        out = jnp.dot(grad, w_in[e], preferred_element_type=F32)
        part[1, chunk["z"][c], :, e] = out.astype(BF16).reshape(RING, count, depth)

    def weight_grad(left, kind, e, target):
        right = rows[kind, :, :, e].reshape(RING * RING * count, depth)
        target[e] = lax.dot_general(left[e], right, (((0,), (0,)), ((), ())),
                                    preferred_element_type=F32).astype(BF16)

    stores = (
        pltpu.make_async_copy(w_in_grad, w_in_grad_ref, store_sem.at[0]),
        pltpu.make_async_copy(w_out_grad, w_out_grad_ref, store_sem.at[1]),
    )

    def swap_in(kind):
        make_slots(kind)
        if kind == 0:
            pl.semaphore_wait(barrier, 4 + group - 1)
        swap_start(kind, 0, outbox, inbox)

    def load_weights():
        for load in loads:
            load.wait()

    tasks["weights",] = load_weights
    for kind in range(2):
        tasks["make", kind] = lambda kind=kind: swap_in(kind)
        tasks["own", kind] = lambda kind=kind: own_rows(kind)
        for p in range(2):
            gather(kind, p)
            reduce(kind, p)
        for c in range(RING):
            for e in range(members):
                tasks["part", kind, c, e] = lambda kind=kind, c=c, e=e: (forward, backward)[kind](c, e)
        tasks["back", kind] = lambda kind=kind: send_back(kind)
        tasks["finish", kind] = lambda kind=kind: finish(kind)
        left, target = ((pre_grad, w_in_grad), (hidden, w_out_grad))[kind]
        for e in range(members):
            tasks["weight", kind, e] = (
                lambda left=left, kind=kind, e=e, target=target: weight_grad(left, kind, e, target))
        tasks["store", kind] = lambda kind=kind: stores[kind].start()

    assert sorted(tasks, key=str) == sorted(ORDER, key=str)
    for name in ORDER:
        tasks[name]()

    for copy in sent:
        copy.wait_send()

    def swapped(by, carry):
        for kind in range(2):
            swap_copy(kind, 0, by, outbox, inbox).wait_send()
            swap_copy(kind, 1, by, back_outbox, back_inbox).wait_send()
        return carry

    lax.fori_loop(1, group, swapped, 0)
    for store in stores:
        store.wait()


def last_kernel(
    tokens, logits_ref, slot_in_grad_ref, from_combine_ref, w_in_grad_ref, w_out_grad_ref,
    token_grad_ref, logit_grad_ref, w_in_out_ref, w_out_out_ref,
    token_grad, sem, token_sem,
):
    images, slots, _ = logits_ref.shape
    moves = [
        pltpu.make_async_copy(source.at[e], target.at[e], sem.at[2 * i + e])
        for i, (source, target) in enumerate(
            ((w_in_grad_ref, w_in_out_ref), (w_out_grad_ref, w_out_out_ref)))
        for e in range(2)
    ]
    for move in moves:
        move.start()
    softs = []
    for image in range(images):
        back = slot_in_grad_ref[image * slots:(image + 1) * slots]
        softs.append(soft_weights(logits_ref[image], 1))
        token_grad[image] = lax.dot_general(
            softs[image].astype(BF16), back, (((0,), (0,)), ((), ())), preferred_element_type=F32
        ).astype(BF16)
        moves.append(pltpu.make_async_copy(token_grad.at[image], token_grad_ref.at[image], token_sem.at[image]))
        moves[-1].start()
    for image in range(images):
        back = slot_in_grad_ref[image * slots:(image + 1) * slots]
        grad = lax.dot_general(back, tokens[image], (((1,), (1,)), ((), ())), preferred_element_type=F32)
        soft = softs[image]
        grad = soft * (grad - jnp.sum(soft * grad, axis=1, keepdims=True))
        logit_grad_ref[image] = from_combine_ref[image] + grad
    for move in moves:
        move.wait()


COPIES = 2 * 2 * 2 * (4 + 4 * RING)


def shards(tokens, logits, out_grad, w_in, w_out):
    images, length, depth = tokens.shape
    slots = logits.shape[2]
    logits = jnp.transpose(logits, (0, 2, 1))
    members, width, _ = w_in.shape
    group = slots // members
    count = group * images
    block = (members, count)
    kept = (members, RING * RING * count, width)
    columns = depth // 2 // TILE
    swapped = (2, group, (columns + columns % 2) * 8, TILE)
    split = (SPLIT, depth - SPLIT)
    shape = jax.ShapeDtypeStruct
    whole = pl.BlockSpec(memory_space=pl.ANY)
    inside = pl.BlockSpec(memory_space=pltpu.VMEM)
    far = pl.BlockSpec(memory_space=pltpu.HBM)
    slot_in_grad, from_combine, w_in_grad, w_out_grad = pl.pallas_call(
        kernel,
        out_shape=(
            shape((images * slots, depth), BF16),
            shape(logits.shape, F32),
            shape(w_in.shape, BF16),
            shape(w_out.shape, BF16),
        ),
        in_specs=[inside, inside, inside, far, far],
        out_specs=(inside, inside, whole, whole),
        scratch_shapes=[
            pltpu.VMEM(logits.shape, F32),
            pltpu.VMEM(swapped, BF16),
            pltpu.VMEM(swapped, BF16),
            pltpu.VMEM(swapped, BF16),
            pltpu.VMEM(swapped, BF16),
            pltpu.VMEM((2, RING, RING) + block + (depth,), BF16),
            pltpu.VMEM((2, RING, RING) + block + (depth,), BF16),
            pltpu.VMEM((2, RING, 2, count, split[0]), BF16),
            pltpu.VMEM((2, RING, 2) + block + (split[0],), BF16),
            pltpu.VMEM((2, RING, 2, count, split[1]), BF16),
            pltpu.VMEM((2, RING, 2) + block + (split[1],), BF16),
            pltpu.VMEM((2, 2, count, depth), BF16),
            pltpu.VMEM((2, 2) + block + (depth,), BF16),
            pltpu.VMEM((2,) + block + (depth,), BF16),
            pltpu.VMEM(w_in.shape, BF16),
            pltpu.VMEM(w_out.shape, BF16),
            pltpu.VMEM(kept, F32),
            pltpu.VMEM(kept, BF16),
            pltpu.VMEM(kept, BF16),
            pltpu.VMEM(w_in.shape, BF16),
            pltpu.VMEM(w_out.shape, BF16),
            pltpu.SemaphoreType.DMA((2,)),
            pltpu.SemaphoreType.DMA((2,)),
            pltpu.SemaphoreType.DMA((2, 2, group)),
            pltpu.SemaphoreType.DMA((2, 2, group)),
            pltpu.SemaphoreType.DMA((COPIES,)),
            pltpu.SemaphoreType.DMA((COPIES,)),
        ],
        compiler_params=pltpu.CompilerParams(
            collective_id=0, has_side_effects=True, vmem_limit_bytes=48 * 2**20
        ),
    )(tokens, logits, out_grad, w_in, w_out)
    token_grad, logit_grad, w_in_grad, w_out_grad = pl.pallas_call(
        last_kernel,
        out_shape=(
            shape(tokens.shape, BF16),
            shape(logits.shape, F32),
            shape(w_in.shape, BF16),
            shape(w_out.shape, BF16),
        ),
        in_specs=[inside, inside, inside, inside, whole, whole],
        out_specs=(whole, inside, whole, whole),
        scratch_shapes=[
            pltpu.VMEM(tokens.shape, BF16),
            pltpu.SemaphoreType.DMA((4,)),
            pltpu.SemaphoreType.DMA((2,)),
        ],
        compiler_params=pltpu.CompilerParams(vmem_limit_bytes=16 * 2**20),
    )(tokens, logits, slot_in_grad, from_combine, w_in_grad, w_out_grad)
    return token_grad, jnp.transpose(logit_grad, (0, 2, 1)), w_in_grad, w_out_grad


def solution(mesh):
    placed = (
        P(("dp", "expert"), None, None),
        P(("dp", "expert"), None, None),
        P(("dp", "expert"), None, None),
        P("expert", "dp", None),
        P("expert", "dp", None),
    )
    return jax.shard_map(
        shards,
        mesh=mesh,
        in_specs=placed,
        out_specs=(
            P(("dp", "expert"), None, None),
            P(("dp", "expert"), None, None),
            P("expert", "dp", None),
            P("expert", "dp", None),
        ),
        check_vma=False,
    )
```

profile of v0, /device:TPU:1, one launch (start us, length us, event | category | flops | bytes accessed | tf_op | source)
XLA Modules:
  0.0 109.3 jit_solution(11556614906419925202)
XLA Ops:
  0.6 0.0 copy-start
  0.6 1.3 %copy-done = bf16[2,256,1280]{2,1,0:T(8,128)(2,1)S(1)} copy-done((bf16[2,256,1280]{2,1,0:T(8,128)(2,1)S(1)}, bf16[2,256,1280]{2,1,0:T(8,128)(2,1)}, u32[]{:S(2)}) %copy-start) | copy-done | bytes 1310744
  1.9 0.0 copy-start.1
  2.0 1.3 %copy-done.1 = bf16[2,256,1280]{2,1,0:T(8,128)(2,1)S(1)} copy-done((bf16[2,256,1280]{2,1,0:T(8,128)(2,1)S(1)}, bf16[2,256,1280]{2,1,0:T(8,128)(2,1)}, u32[]{:S(2)}) %copy-start.1) | copy-done | bytes 1310744
  3.3 0.0 copy-start.2
  3.3 0.8 copy-done.2
  4.1 102.1 %shard_map.84 = (bf16[64,1280]{1,0:T(8,128)(2,1)S(1)}, f32[2,32,256]{2,1,0:T(8,128)S(1)}, bf16[2,320,1280]{2,1,0:T(8,128)(2,1)S(1)}, bf16[2,320,1280]{2,1,0:T(8,128)(2,1)S(1)}) custom-call(bf16[2,256,1280]{2,1,0:T(8,128)(2,1)S(1)} %copy-done, f32[2,32,256]{2,1,0:T(8,128)S(1)} %bitcast.2, bf16[2,256,1280]{2,1,0:T(8,128)(2,1)S(1)} %copy-done.1, ...), custom_call_target="tpu_custom_call" | custom-call | tf_op jit(solution)/shard_map/pallas_call | solution.py:489
  106.2 3.1 %shard_map.85 = (bf16[2,256,1280]{2,1,0:T(8,128)(2,1)}, f32[2,32,256]{2,1,0:T(8,128)}, bf16[2,320,1280]{2,1,0:T(8,128)(2,1)}, bf16[2,320,1280]{2,1,0:T(8,128)(2,1)}) custom-call(bf16[2,256,1280]{2,1,0:T(8,128)(2,1)S(1)} %copy-done, f32[2,32,256]{2,1,0:T(8,128)S(1)} %bitcast.3, bf16[64,1280]{1,0:T(8,128)(2,1)S(1)} %get-tuple-element.12.slot_in_grad_ref, ...), custom_call_target="tpu_custom_call" | custom-call | tf_op jit(solution)/shard_map/pallas_call | solution.py:532
Async XLA Ops:
  0.6 1.3 %copy-start = (bf16[2,256,1280]{2,1,0:T(8,128)(2,1)S(1)}, bf16[2,256,1280]{2,1,0:T(8,128)(2,1)}, u32[]{:S(2)}) copy-start(bf16[2,256,1280]{2,1,0:T(8,128)(2,1)} %tokens.3) | copy-start | bytes 3932164
  1.9 1.3 %copy-start.1 = (bf16[2,256,1280]{2,1,0:T(8,128)(2,1)S(1)}, bf16[2,256,1280]{2,1,0:T(8,128)(2,1)}, u32[]{:S(2)}) copy-start(bf16[2,256,1280]{2,1,0:T(8,128)(2,1)} %out_grad.1) | copy-start | bytes 3932164
  3.3 0.8 copy-start.2
where the time goes:
time: 110 us; the launch traced here: 109 us
  Pallas kernels  105 us (95%)
  local copies, waits for them, and re-layouts  3.46 us (3%)
    pallas_call x1, Pallas kernels, shards(): pl.pallas_call(kernel, out_shape=(shape((images * slots, depth), BF16), s...  102 us
    unnamed x6, local copies, waits for them, and re-layouts  3.46 us
    pallas_call x1, Pallas kernels, shards(): pl.pallas_call(last_kernel, out_shape=(shape(tokens.shape, BF16), shape(l...  3.1 us

commit v1 on v0

v1 whole, which is shorter than its diff:
```python
import jax
import jax.numpy as jnp
from jax import lax
from jax.experimental import pallas as pl
from jax.experimental.pallas import tpu as pltpu
from jax.sharding import PartitionSpec as P

RING = 4
TILE = 128
SPLIT = 768
PIECES = 5
COPIES = 2 * 74 + 4 * PIECES
MESH = pl.DeviceIdType.MESH
BF16 = jnp.bfloat16
F32 = jnp.float32


def normal_cdf(values):
    return 0.5 * (1.0 + lax.erf(values * 0.7071067811865476))


def soft_weights(values, over_dim):
    highest = jnp.max(values, axis=over_dim, keepdims=True)
    raised = jnp.exp(values - highest)
    return raised / jnp.sum(raised, axis=over_dim, keepdims=True)


def shift(at, by, size):
    return lax.rem(at + (by + size), size)


def iota(shape, dim):
    return lax.broadcasted_iota(jnp.int32, shape, dim)


def zero_one(mask):
    return mask.astype(F32).astype(BF16)


def tiled(block, group):
    packed, features = block.shape
    pieces = [
        block[:, at * TILE:(at + 1) * TILE].reshape(group, 1, packed // group, TILE)
        for at in range(features // TILE)
    ]
    if len(pieces) % 2:
        pieces.append(jnp.zeros_like(pieces[0]))
    block = jnp.concatenate(pieces, axis=1)
    return block.reshape(group, len(pieces) * (packed // group), TILE).astype(BF16)


def untiled(block, features):
    group, high, _ = block.shape
    block = block.astype(F32).reshape(group, high // 8, 8, TILE)
    return jnp.concatenate(
        [block[:, at].reshape(group * 8, TILE) for at in range(features // TILE)], axis=1
    ).astype(BF16)


def picker(packed, half, by_member, lead):
    shape = (packed // 2, packed)
    row, column = iota(shape, 0), iota(shape, 1)
    first, source, second = row // (packed // 4), (row % (packed // 4)) // 2, row % 2
    image, member = (second, (first + lead) % 2) if by_member else (first, second)
    return zero_one(column == ((source * 2 + half) * 2 + image) * 2 + member)


def unpack(block, depth, by_member, lead=0):
    block = untiled(block, depth // 2)
    return jnp.concatenate(
        [jnp.dot(picker(block.shape[0], half, by_member, lead), block, preferred_element_type=F32)
         for half in range(2)],
        axis=1,
    ).astype(BF16)


def pack(block, lead):
    rows, depth = block.shape
    return sum(
        lax.dot_general(picker(2 * rows, half, True, lead), block[:, half * depth // 2:(half + 1) * depth // 2],
                        (((0,), (0,)), ((), ())), preferred_element_type=F32)
        for half in range(2)
    )


ORDER = (
    ("enter",), ("make", 0), ("ws", 3), ("ws", 2), ("make", 1), ("ws", 0), ("ws", 8), ("own", 0), ("z1", 0, 0),
    ("g1", 0), ("b1", 0), ("ws", 9), ("own", 1), ("b1", 1), ("ws", 6), ("z1", 1, 0), ("b2t", 0), ("z1", 0, 1),
    ("ws", 5), ("z2t", 0, 0, 0), ("z1", 0, 2), ("ws", 4), ("g2t", 0, 1), ("g2t", 0, 0), ("ws", 7), ("z1", 0, 3),
    ("s1", 0, 0), ("z2t", 1, 0, 1), ("s1", 0, 2), ("z2t", 0, 1, 0), ("z2t", 0, 2, 1), ("s1", 0, 1),
    ("z2t", 1, 0, 0), ("z2t", 0, 1, 1), ("z2t", 0, 2, 0), ("z1", 1, 2), ("ws", 1), ("z2t", 0, 3, 1),
    ("s2t", 0, 0), ("z2t", 0, 3, 0), ("z2t", 0, 0, 1), ("s1", 0, 3), ("g1", 1), ("zg", 0, 1), ("zg", 1, 0),
    ("s2t", 0, 2), ("zg", 0, 2), ("s2t", 0, 1), ("b2t", 1), ("s1", 1, 0), ("weights",), ("g", 0, 0),
    ("zg", 0, 3), ("zg", 0, 0), ("part", 0, 0), ("z2t", 1, 2, 1), ("z2t", 1, 2, 0), ("z1", 1, 1), ("s2t", 0, 3),
    ("r1", 0, 0), ("g", 0, 1), ("part", 0, 1), ("r1", 0, 1), ("z1", 1, 3), ("s2t", 1, 0), ("g", 0, 2),
    ("part", 0, 2), ("zg", 1, 2), ("g2t", 1, 1), ("g2t", 1, 0), ("r2t", 0, 0), ("s1", 1, 2), ("g", 0, 3),
    ("part", 0, 3), ("z2t", 1, 1, 1), ("r2t", 0, 1), ("q1", 0, 1), ("q1", 0, 0), ("r1", 0, 3), ("r1", 0, 2),
    ("g", 1, 0), ("z2t", 1, 1, 0), ("r", 0, 0), ("s1", 1, 1), ("z2t", 1, 3, 1), ("z2t", 1, 3, 0), ("q1", 0, 3),
    ("s2t", 1, 2), ("r", 0, 1), ("q1", 0, 2), ("s1", 1, 3), ("q2t", 0, 1, 0), ("r2t", 0, 3), ("q2t", 0, 1, 1),
    ("r2t", 0, 2), ("zg", 1, 1), ("q2t", 0, 0, 0), ("q2t", 0, 0, 1), ("zg", 1, 3), ("part", 1, 0),
    ("s2t", 1, 1), ("q2t", 0, 3, 0), ("q2t", 0, 3, 1), ("g", 1, 2), ("part", 1, 2), ("s2t", 1, 3), ("r", 0, 3),
    ("q", 0, 1), ("q2t", 0, 2, 0), ("r1", 1, 2), ("q2t", 0, 2, 1), ("r1", 1, 0), ("t1", 0), ("r", 0, 2),
    ("g", 1, 1), ("part", 1, 1), ("r1", 1, 1), ("q", 0, 0), ("g", 1, 3), ("part", 1, 3), ("q1", 1, 2),
    ("r1", 1, 3), ("r2t", 1, 0), ("q", 0, 3), ("q1", 1, 1), ("r2t", 1, 2), ("q1", 1, 3), ("weight", 0),
    ("r2t", 1, 1), ("t2t", 0, 1), ("t2t", 0, 0), ("ds", 0, 2), ("q", 0, 2), ("weight", 1), ("r2t", 1, 3),
    ("v1", 0), ("r", 1, 0), ("r", 1, 2), ("ds", 1, 1), ("r", 1, 1), ("q2t", 1, 3, 1), ("q2t", 1, 3, 0),
    ("ds", 0, 3), ("q2t", 1, 2, 1), ("q2t", 1, 2, 0), ("r", 1, 3), ("t1", 1), ("v2t", 0), ("ds", 1, 2),
    ("t", 0), ("q1", 1, 0), ("q", 1, 3), ("ds", 1, 3), ("q2t", 1, 1, 1), ("q2t", 1, 1, 0), ("q", 1, 2),
    ("v", 0), ("back", 0), ("v1", 1), ("ds", 1, 4), ("t2t", 1, 1), ("t2t", 1, 0), ("ds", 1, 0), ("q", 1, 1),
    ("v2t", 1), ("q2t", 1, 0, 1), ("ds", 0, 0), ("q2t", 1, 0, 0), ("finish", 0), ("ds", 0, 1), ("store", 1),
    ("t", 1), ("ds", 0, 4), ("q", 1, 0), ("v", 1), ("back", 1), ("store", 0), ("finish", 1),
)


def kernel(
    tokens, logits_ref, out_grad, w_in_ref, w_out_ref,
    slot_in_grad_ref, from_combine_ref, w_in_grad_ref, w_out_grad_ref,
    combine, outbox, inbox, back_outbox, back_inbox,
    rows, other, part, other_part, from_twin, last_half, last_full, side_half, side_full, side_twin, total,
    weights, weight_grads, mate_grads, slope, hidden, pre_grad,
    load_sem, store_sem, swap_send, swap_recv, send_sem, recv_sem,
):
    count, depth = rows.shape[3:]
    width = weights.shape[1] // 2
    images, slots, length = combine.shape
    members = 2
    group = slots // members
    packed = group * 2 * images * members
    me = lax.axis_index("dp")
    mine = lax.axis_index("expert")
    z, x = me // RING, lax.rem(me, RING)
    z_to = (shift(z, 1, RING), shift(z, -1, RING))
    z_from = (z_to[1], z_to[0])
    chunk = (z, z_from[0], z_from[1], shift(z, 2, RING))
    z_dev = tuple(to * RING + x for to in z_to)
    turn = lax.rem(mine, 2)
    turned = shift(x, turn, RING)
    mate = shift(turned + 1 - 2 * lax.rem(turned, 2), RING - turn, RING)
    twin = shift(RING - 1 - turned, RING - turn, RING)
    beyond = shift(x, 2, RING)
    places = (x, mate, twin, beyond)
    mate_dev, twin_dev = z * RING + mate, z * RING + twin
    own = lax.rem((turned + 1) // 2, 2)
    first, second = pl.ds(0, SPLIT), pl.ds(SPLIT, depth - SPLIT)
    halves = (pl.ds(0, count // 2), pl.ds(count // 2, count // 2))

    def partner(by):
        return lax.rem(mine + by, group)

    barrier = pltpu.get_barrier_semaphore()
    for there in z_dev + (mate_dev, twin_dev):
        pl.semaphore_signal(barrier, inc=1, device_id={"dp": there}, device_id_type=MESH)

    def greet(by, carry):
        pl.semaphore_signal(barrier, inc=1, device_id={"expert": partner(by)}, device_id_type=MESH)
        return carry

    lax.fori_loop(1, group, greet, 0)

    loads = [
        pltpu.make_async_copy(source.at[own], weights.at[i, pl.ds(0, width)], load_sem.at[i])
        for i, source in enumerate((w_in_ref, w_out_ref))
    ]
    for load in loads:
        load.start()

    def swap_copy(kind, way, by, box, inbound):
        return pltpu.make_async_remote_copy(
            src_ref=box.at[kind, partner(by)], dst_ref=inbound.at[kind, mine],
            send_sem=swap_send.at[way, kind, by], recv_sem=swap_recv.at[way, kind, by],
            device_id={"expert": partner(by)}, device_id_type=MESH,
        )

    def swap_start(kind, way, box, inbound):
        def one(by, carry):
            swap_copy(kind, way, by, box, inbound).start()
            return carry

        lax.fori_loop(1, group, one, 0)
        inbound[kind, mine] = box[kind, mine]

    def swap_arrived(kind, way, box, inbound):
        def one(by, carry):
            swap_copy(kind, way, by, box, inbound).wait_recv()
            return carry

        lax.fori_loop(1, group, one, 0)

    def make_slots(kind):
        source = (tokens, out_grad)[kind]
        left = []
        for image in range(images):
            soft = soft_weights(logits_ref[image], 1 - kind)
            if kind == 1:
                combine[image] = soft
            row, slot = iota((packed, slots), 0), iota((packed, slots), 1)
            spread = zero_one((slot == (row // 8) * 2 + row % 2) & ((row // 2) % 2 == image))
            left.append(jnp.dot(spread, soft.astype(BF16), preferred_element_type=F32).astype(BF16))
        slot = jnp.dot(jnp.concatenate(left, axis=1), source[...].reshape(images * length, depth),
                       preferred_element_type=F32)
        first = (iota((packed, depth // 2), 0) // 4) % 2 == 0
        outbox[kind] = tiled(jnp.where(first, slot[:, :depth // 2], slot[:, depth // 2:]), group)

    def own_rows(kind):
        swap_arrived(kind, 0, outbox, inbox)
        block = unpack(inbox[kind], depth, True, own)
        rows[kind, z, x] = block[:count]
        other[kind, z] = block[count:]

    def send_back(kind):
        back_outbox[kind] = tiled(pack(total[kind].reshape(members * count, depth), own), group)
        swap_start(kind, 1, back_outbox, back_inbox)

    def finish(kind):
        swap_arrived(kind, 1, back_outbox, back_inbox)
        back = unpack(back_inbox[kind], depth, False)
        if kind == 1:
            slot_in_grad_ref[...] = back
            return
        for image in range(images):
            grad = lax.dot_general(back[image * slots:(image + 1) * slots], out_grad[image],
                                   (((1,), (1,)), ((), ())), preferred_element_type=F32)
            soft = combine[image]
            from_combine_ref[image] = soft * (grad - jnp.sum(soft * grad, axis=0, keepdims=True))

    sent = []
    flying = {}

    def send(key, source, target, there):
        copy = pltpu.make_async_remote_copy(
            src_ref=source, dst_ref=target,
            send_sem=send_sem.at[len(sent)], recv_sem=recv_sem.at[len(sent)],
            device_id={"dp": there}, device_id_type=MESH,
        )
        copy.start()
        sent.append(copy)
        flying[key] = copy

    def arrived(*key):
        flying.pop(key).wait_recv()

    tasks = {}

    def task(*name):
        def keep(run):
            tasks[name] = run
            return run

        return keep

    def gather(kind):
        def z_pieces(at):
            return rows.at[kind, at, x, :, first], other.at[kind, at, :, first]

        @task("g1", kind)
        def _():
            for way in range(2):
                for i, piece in enumerate(z_pieces(z)):
                    send(("g1", kind, way, i), piece, piece, z_dev[way])

        for way in range(2):
            @task("g2t", kind, way)
            def _(way=way):
                for i in range(2):
                    arrived("g1", kind, way, i)
                piece = z_pieces(z_from[way])[way]
                send(("g2", kind, way), piece, piece, z_dev[way])

        def along_x(name, at, features):
            here = rows.at[kind, at, x, :, features]
            send(name + ("twin",), here, here, twin_dev)
            send(name + ("mate",), other.at[kind, at, :, features], here, mate_dev)

        def from_mate(name, at, features):
            arrived(*name, "mate")
            piece = rows.at[kind, at, mate, :, features]
            send(name + ("beyond",), piece, piece, twin_dev)

        for c in range(RING):
            @task("s1", kind, c)
            def _(c=c):
                if c == 3:
                    for way in range(2):
                        arrived("g2", kind, way)
                along_x(("s1", kind, c), chunk[c], first)

            @task("s2t", kind, c)
            def _(c=c):
                from_mate(("s1", kind, c), chunk[c], first)

            @task("g", kind, c)
            def _(c=c):
                arrived("s1", kind, c, "twin")
                arrived("s1", kind, c, "beyond")

        @task("b1", kind)
        def _():
            along_x(("b1", kind), z, second)

        @task("b2t", kind)
        def _():
            from_mate(("b1", kind), z, second)

        for c in range(RING):
            @task("z1", kind, c)
            def _(c=c):
                if c >= 2:
                    arrived("b1", kind, ("twin", "beyond")[c - 2])
                piece = rows.at[kind, z, places[c], :, second]
                for way in range(2):
                    send(("z1", kind, c, way), piece, piece, z_dev[way])

            for way in range(2):
                @task("z2t", kind, c, way)
                def _(c=c, way=way):
                    arrived("z1", kind, c, way)
                    piece = rows.at[kind, z_from[way], places[c], halves[way], second]
                    send(("z2", kind, c, way), piece, piece, z_dev[way])

            @task("zg", kind, c)
            def _(c=c):
                for way in range(2):
                    arrived("z2", kind, c, way)

    def plus(*refs):
        value = refs[0][...].astype(F32)
        for ref in refs[1:]:
            value = value + ref[...].astype(F32)
        return value.astype(BF16)

    def reduce(kind):
        def to_twin(name, at, features, boxes):
            for i, place in enumerate((beyond, twin)):
                send(name + (i,), part.at[kind, at, place, :, features], boxes.at[i], twin_dev)

        def to_mate(name, at, features, boxes):
            arrived(*name, 0)
            piece = part.at[kind, at, mate, :, features]
            piece[...] = plus(piece, boxes.at[0])
            send(name + ("mate",), piece, other_part.at[kind, at, :, features], mate_dev)

        for c in range(RING):
            @task("r1", kind, c)
            def _(c=c):
                to_twin(("r1", kind, c), chunk[c], first, from_twin.at[kind, c])

            @task("r2t", kind, c)
            def _(c=c):
                to_mate(("r1", kind, c), chunk[c], first, from_twin.at[kind, c])

            @task("r", kind, c)
            def _(c=c):
                arrived("r1", kind, c, 1)
                arrived("r1", kind, c, "mate")
                piece = part.at[kind, chunk[c], x, :, first]
                piece[...] = plus(piece, from_twin.at[kind, c, 1])

        def z_pieces(at):
            return part.at[kind, at, x, :, first], other_part.at[kind, at, :, first]

        @task("t1", kind)
        def _():
            for way, piece in enumerate(z_pieces(chunk[3])):
                send(("t1", kind, way), piece, last_half.at[kind, way], z_dev[way])

        for way in range(2):
            @task("t2t", kind, way)
            def _(way=way):
                arrived("t1", kind, way)
                pieces = z_pieces(z_to[way])
                pieces[way][...] = plus(pieces[way], last_half.at[kind, way])
                for i, piece in enumerate(pieces):
                    send(("t2", kind, way, i), piece, last_full.at[kind, way, i], z_dev[way])

        @task("t", kind)
        def _():
            for i, piece in enumerate(z_pieces(z)):
                for way in range(2):
                    arrived("t2", kind, way, i)
                total[kind, i, :, first] = plus(piece, last_full.at[kind, 0, i], last_full.at[kind, 1, i])

        for c in range(RING):
            @task("q1", kind, c)
            def _(c=c):
                for way in range(2):
                    send(("q1", kind, c, way), part.at[kind, chunk[3], places[c], halves[way], second],
                         side_half.at[kind, c, way], z_dev[way])

            for way in range(2):
                @task("q2t", kind, c, way)
                def _(c=c, way=way):
                    arrived("q1", kind, c, way)
                    piece = part.at[kind, z_to[way], places[c], halves[way], second]
                    piece[...] = plus(piece, side_half.at[kind, c, way])
                    send(("q2", kind, c, way), part.at[kind, z_to[way], places[c], :, second],
                         side_full.at[kind, c, way], z_dev[way])

            @task("q", kind, c)
            def _(c=c):
                for way in range(2):
                    arrived("q2", kind, c, way)
                piece = part.at[kind, z, places[c], :, second]
                piece[...] = plus(piece, side_full.at[kind, c, 0], side_full.at[kind, c, 1])

        @task("v1", kind)
        def _():
            to_twin(("v1", kind), z, second, side_twin.at[kind])

        @task("v2t", kind)
        def _():
            to_mate(("v1", kind), z, second, side_twin.at[kind])

        @task("v", kind)
        def _():
            arrived("v1", kind, 1)
            arrived("v1", kind, "mate")
            total[kind, 0, :, second] = plus(part.at[kind, z, x, :, second], side_twin.at[kind, 1])
            total[kind, 1, :, second] = other_part[kind, z, :, second]

    def chunk_rows(kind, c):
        return rows[kind, chunk[c]].reshape(RING * count, depth)

    def place(c):
        return pl.ds(pl.multiple_of(chunk[c] * (RING * count), RING * count), RING * count)

    def forward(c):
        pre = lax.dot_general(chunk_rows(0, c), weights[0], (((1,), (1,)), ((), ())),
                              preferred_element_type=F32)
        cdf = normal_cdf(pre)
        act = (pre * cdf).astype(BF16)
        slope[place(c)] = cdf + pre * jnp.exp(-0.5 * pre * pre) * 0.3989422804014327
        hidden[place(c)] = act
        out = jnp.dot(act, weights[1], preferred_element_type=F32)
        part[0, chunk[c]] = out.astype(BF16).reshape(RING, count, depth)

    def backward(c):
        grad = lax.dot_general(chunk_rows(1, c), weights[1], (((1,), (1,)), ((), ())),
                               preferred_element_type=F32)
        grad = (grad * slope[place(c)]).astype(BF16)
        pre_grad[place(c)] = grad
        out = jnp.dot(grad, weights[0], preferred_element_type=F32)
        part[1, chunk[c]] = out.astype(BF16).reshape(RING, count, depth)

    def weight_grad(kind):
        left = (pre_grad, hidden)[kind][...]
        for part_at in range(2):
            columns = pl.ds(part_at * (depth // 2), depth // 2)
            right = rows[kind, :, :, :, columns].reshape(RING * RING * count, depth // 2)
            weight_grads[kind, :, columns] = lax.dot_general(
                left, right, (((0,), (0,)), ((), ())), preferred_element_type=F32).astype(BF16)

    piece_rows = width // PIECES

    def weight_piece(i):
        matrix, at = i // PIECES, i % PIECES * piece_rows
        send(("w", i), (w_in_ref, w_out_ref)[matrix].at[1 - own, pl.ds(at, piece_rows)],
             weights.at[matrix, pl.ds(width + at, piece_rows)], mate_dev)

    def grad_piece(kind, i):
        at = i * piece_rows
        send(("d", kind, i), weight_grads.at[kind, pl.ds(width + at, piece_rows)],
             mate_grads.at[kind, pl.ds(at, piece_rows)], mate_dev)

    outs = (w_in_grad_ref, w_out_grad_ref)
    stores = []

    def store(kind):
        for i in range(PIECES):
            arrived("d", kind, i)
        for i, source in enumerate((weight_grads.at[kind, pl.ds(0, width)], mate_grads.at[kind])):
            stores.append(pltpu.make_async_copy(
                source, outs[kind].at[(own, 1 - own)[i]], store_sem.at[kind, i]))
            stores[-1].start()

    @task("enter")
    def _():
        make_slots(0)
        pl.semaphore_wait(barrier, 4 + group - 1)

    @task("weights")
    def _():
        for i in range(2 * PIECES):
            arrived("w", i)
        for load in loads:
            load.wait()

    for i in range(2 * PIECES):
        tasks["ws", i] = lambda i=i: weight_piece(i)
    for kind in range(2):
        @task("make", kind)
        def _(kind=kind):
            if kind == 1:
                make_slots(1)
            swap_start(kind, 0, outbox, inbox)

        tasks["own", kind] = lambda kind=kind: own_rows(kind)
        gather(kind)
        reduce(kind)
        for c in range(RING):
            tasks["part", kind, c] = lambda kind=kind, c=c: (forward, backward)[kind](c)
        tasks["back", kind] = lambda kind=kind: send_back(kind)
        tasks["finish", kind] = lambda kind=kind: finish(kind)
        tasks["weight", kind] = lambda kind=kind: weight_grad(kind)
        for i in range(PIECES):
            tasks["ds", kind, i] = lambda kind=kind, i=i: grad_piece(kind, i)
        tasks["store", kind] = lambda kind=kind: store(kind)

    assert sorted(tasks, key=str) == sorted(ORDER, key=str)
    for name in ORDER:
        tasks[name]()
    assert not flying and len(sent) == COPIES

    for copy in sent:
        copy.wait_send()

    def swapped(by, carry):
        for kind in range(2):
            swap_copy(kind, 0, by, outbox, inbox).wait_send()
            swap_copy(kind, 1, by, back_outbox, back_inbox).wait_send()
        return carry

    lax.fori_loop(1, group, swapped, 0)
    for copy in stores:
        copy.wait()


def last_kernel(
    tokens, logits_ref, slot_in_grad_ref, from_combine_ref, w_in_grad_ref, w_out_grad_ref,
    token_grad_ref, logit_grad_ref, w_in_out_ref, w_out_out_ref,
    token_grad, sem, token_sem,
):
    images, slots, _ = logits_ref.shape
    moves = [
        pltpu.make_async_copy(source.at[e], target.at[e], sem.at[2 * i + e])
        for i, (source, target) in enumerate(
            ((w_in_grad_ref, w_in_out_ref), (w_out_grad_ref, w_out_out_ref)))
        for e in range(2)
    ]
    for move in moves:
        move.start()
    softs = []
    for image in range(images):
        back = slot_in_grad_ref[image * slots:(image + 1) * slots]
        softs.append(soft_weights(logits_ref[image], 1))
        token_grad[image] = lax.dot_general(
            softs[image].astype(BF16), back, (((0,), (0,)), ((), ())), preferred_element_type=F32
        ).astype(BF16)
        moves.append(pltpu.make_async_copy(token_grad.at[image], token_grad_ref.at[image], token_sem.at[image]))
        moves[-1].start()
    for image in range(images):
        back = slot_in_grad_ref[image * slots:(image + 1) * slots]
        grad = lax.dot_general(back, tokens[image], (((1,), (1,)), ((), ())), preferred_element_type=F32)
        soft = softs[image]
        grad = soft * (grad - jnp.sum(soft * grad, axis=1, keepdims=True))
        logit_grad_ref[image] = from_combine_ref[image] + grad
    for move in moves:
        move.wait()


def shards(tokens, logits, out_grad, w_in, w_out):
    images, length, depth = tokens.shape
    slots = logits.shape[2]
    logits = jnp.transpose(logits, (0, 2, 1))
    members, width, _ = w_in.shape
    group = slots // members
    count = group * images
    kept = (RING * RING * count, 2 * width)
    columns = depth // 2 // TILE
    swapped = (2, group, (columns + columns % 2) * 8, TILE)
    rest = depth - SPLIT
    shape = jax.ShapeDtypeStruct
    whole = pl.BlockSpec(memory_space=pl.ANY)
    inside = pl.BlockSpec(memory_space=pltpu.VMEM)
    far = pl.BlockSpec(memory_space=pltpu.HBM)
    slot_in_grad, from_combine, w_in_grad, w_out_grad = pl.pallas_call(
        kernel,
        out_shape=(
            shape((images * slots, depth), BF16),
            shape(logits.shape, F32),
            shape(w_in.shape, BF16),
            shape(w_out.shape, BF16),
        ),
        in_specs=[inside, inside, inside, far, far],
        out_specs=(inside, inside, whole, whole),
        scratch_shapes=[
            pltpu.VMEM(logits.shape, F32),
            pltpu.VMEM(swapped, BF16),
            pltpu.VMEM(swapped, BF16),
            pltpu.VMEM(swapped, BF16),
            pltpu.VMEM(swapped, BF16),
            pltpu.VMEM((2, RING, RING, count, depth), BF16),
            pltpu.VMEM((2, RING, count, depth), BF16),
            pltpu.VMEM((2, RING, RING, count, depth), BF16),
            pltpu.VMEM((2, RING, count, depth), BF16),
            pltpu.VMEM((2, RING, 2, count, SPLIT), BF16),
            pltpu.VMEM((2, 2, count, SPLIT), BF16),
            pltpu.VMEM((2, 2, 2, count, SPLIT), BF16),
            pltpu.VMEM((2, RING, 2, count // 2, rest), BF16),
            pltpu.VMEM((2, RING, 2, count, rest), BF16),
            pltpu.VMEM((2, 2, count, rest), BF16),
            pltpu.VMEM((2, 2, count, depth), BF16),
            pltpu.VMEM((2, 2 * width, depth), BF16),
            pltpu.VMEM((2, 2 * width, depth), BF16),
            pltpu.VMEM((2, width, depth), BF16),
            pltpu.VMEM(kept, F32),
            pltpu.VMEM(kept, BF16),
            pltpu.VMEM(kept, BF16),
            pltpu.SemaphoreType.DMA((2,)),
            pltpu.SemaphoreType.DMA((2, 2)),
            pltpu.SemaphoreType.DMA((2, 2, group)),
            pltpu.SemaphoreType.DMA((2, 2, group)),
            pltpu.SemaphoreType.DMA((COPIES,)),
            pltpu.SemaphoreType.DMA((COPIES,)),
        ],
        compiler_params=pltpu.CompilerParams(
            collective_id=0, has_side_effects=True, vmem_limit_bytes=48 * 2**20
        ),
    )(tokens, logits, out_grad, w_in, w_out)
    token_grad, logit_grad, w_in_grad, w_out_grad = pl.pallas_call(
        last_kernel,
        out_shape=(
            shape(tokens.shape, BF16),
            shape(logits.shape, F32),
            shape(w_in.shape, BF16),
            shape(w_out.shape, BF16),
        ),
        in_specs=[inside, inside, inside, inside, whole, whole],
        out_specs=(whole, inside, whole, whole),
        scratch_shapes=[
            pltpu.VMEM(tokens.shape, BF16),
            pltpu.SemaphoreType.DMA((4,)),
            pltpu.SemaphoreType.DMA((2,)),
        ],
        compiler_params=pltpu.CompilerParams(vmem_limit_bytes=16 * 2**20),
    )(tokens, logits, slot_in_grad, from_combine, w_in_grad, w_out_grad)
    return token_grad, jnp.transpose(logit_grad, (0, 2, 1)), w_in_grad, w_out_grad


def solution(mesh):
    placed = (
        P(("dp", "expert"), None, None),
        P(("dp", "expert"), None, None),
        P(("dp", "expert"), None, None),
        P("expert", "dp", None),
        P("expert", "dp", None),
    )
    return jax.shard_map(
        shards,
        mesh=mesh,
        in_specs=placed,
        out_specs=(
            P(("dp", "expert"), None, None),
            P(("dp", "expert"), None, None),
            P("expert", "dp", None),
            P("expert", "dp", None),
        ),
        check_vma=False,
    )
```

time: 110 us -> 101 us (0.918)
  Pallas kernels: 105 us -> 97.1 us
    pallas_call x1, Pallas kernels: 102 us -> 94 us  [shards(): pl.pallas_call(kernel, out_shape=(shape((images * slots, depth), BF16), s...]
where the time goes in v1:
time: 101 us
  Pallas kernels  97.1 us (96%)
  local copies, waits for them, and re-layouts  3.46 us (3%)
    pallas_call x1, Pallas kernels, shards(): pl.pallas_call(kernel, out_shape=(shape((images * slots, depth), BF16), s...  94 us
    unnamed x6, local copies, waits for them, and re-layouts  3.46 us
    pallas_call x1, Pallas kernels, shards(): pl.pallas_call(last_kernel, out_shape=(shape(tokens.shape, BF16), shape(l...  3.11 us

profile of v1, /device:TPU:1, one launch (start us, length us, event | category | flops | bytes accessed | tf_op | source)
XLA Modules:
  0.0 101.2 jit_solution(4595165890630823423)
XLA Ops:
  0.6 0.0 copy-start
  0.6 1.3 %copy-done = bf16[2,256,1280]{2,1,0:T(8,128)(2,1)S(1)} copy-done((bf16[2,256,1280]{2,1,0:T(8,128)(2,1)S(1)}, bf16[2,256,1280]{2,1,0:T(8,128)(2,1)}, u32[]{:S(2)}) %copy-start) | copy-done | bytes 1310744
  1.9 0.0 copy-start.1
  2.0 1.3 %copy-done.1 = bf16[2,256,1280]{2,1,0:T(8,128)(2,1)S(1)} copy-done((bf16[2,256,1280]{2,1,0:T(8,128)(2,1)S(1)}, bf16[2,256,1280]{2,1,0:T(8,128)(2,1)}, u32[]{:S(2)}) %copy-start.1) | copy-done | bytes 1310744
  3.3 0.0 copy-start.2
  3.3 0.8 copy-done.2
  4.1 94.0 %shard_map.84 = (bf16[64,1280]{1,0:T(8,128)(2,1)S(1)}, f32[2,32,256]{2,1,0:T(8,128)S(1)}, bf16[2,320,1280]{2,1,0:T(8,128)(2,1)S(1)}, bf16[2,320,1280]{2,1,0:T(8,128)(2,1)S(1)}) custom-call(bf16[2,256,1280]{2,1,0:T(8,128)(2,1)S(1)} %copy-done, f32[2,32,256]{2,1,0:T(8,128)S(1)} %bitcast.2, bf16[2,256,1280]{2,1,0:T(8,128)(2,1)S(1)} %copy-done.1, ...), custom_call_target="tpu_custom_call" | custom-call | tf_op jit(solution)/shard_map/pallas_call | solution.py:575
  98.1 3.1 %shard_map.85 = (bf16[2,256,1280]{2,1,0:T(8,128)(2,1)}, f32[2,32,256]{2,1,0:T(8,128)}, bf16[2,320,1280]{2,1,0:T(8,128)(2,1)}, bf16[2,320,1280]{2,1,0:T(8,128)(2,1)}) custom-call(bf16[2,256,1280]{2,1,0:T(8,128)(2,1)S(1)} %copy-done, f32[2,32,256]{2,1,0:T(8,128)S(1)} %bitcast.3, bf16[64,1280]{1,0:T(8,128)(2,1)S(1)} %get-tuple-element.12.slot_in_grad_ref, ...), custom_call_target="tpu_custom_call" | custom-call | tf_op jit(solution)/shard_map/pallas_call | solution.py:619
Async XLA Ops:
  0.6 1.3 %copy-start = (bf16[2,256,1280]{2,1,0:T(8,128)(2,1)S(1)}, bf16[2,256,1280]{2,1,0:T(8,128)(2,1)}, u32[]{:S(2)}) copy-start(bf16[2,256,1280]{2,1,0:T(8,128)(2,1)} %tokens.3) | copy-start | bytes 3932164
  1.9 1.3 %copy-start.1 = (bf16[2,256,1280]{2,1,0:T(8,128)(2,1)S(1)}, bf16[2,256,1280]{2,1,0:T(8,128)(2,1)}, u32[]{:S(2)}) copy-start(bf16[2,256,1280]{2,1,0:T(8,128)(2,1)} %out_grad.1) | copy-start | bytes 3932164
  3.3 0.8 copy-start.2

commit v2 on v1

--- a/solution.py
+++ b/solution.py
@@ -8,6 +8,7 @@
 RING = 4
 TILE = 128
 SPLIT = 768
+LAG = 90
 PIECES = 5
 COPIES = 2 * 74 + 4 * PIECES
 MESH = pl.DeviceIdType.MESH
@@ -84,31 +85,31 @@
 
 
 ORDER = (
-    ("enter",), ("make", 0), ("ws", 3), ("ws", 2), ("make", 1), ("ws", 0), ("ws", 8), ("own", 0), ("z1", 0, 0),
-    ("g1", 0), ("b1", 0), ("ws", 9), ("own", 1), ("b1", 1), ("ws", 6), ("z1", 1, 0), ("b2t", 0), ("z1", 0, 1),
-    ("ws", 5), ("z2t", 0, 0, 0), ("z1", 0, 2), ("ws", 4), ("g2t", 0, 1), ("g2t", 0, 0), ("ws", 7), ("z1", 0, 3),
-    ("s1", 0, 0), ("z2t", 1, 0, 1), ("s1", 0, 2), ("z2t", 0, 1, 0), ("z2t", 0, 2, 1), ("s1", 0, 1),
-    ("z2t", 1, 0, 0), ("z2t", 0, 1, 1), ("z2t", 0, 2, 0), ("z1", 1, 2), ("ws", 1), ("z2t", 0, 3, 1),
-    ("s2t", 0, 0), ("z2t", 0, 3, 0), ("z2t", 0, 0, 1), ("s1", 0, 3), ("g1", 1), ("zg", 0, 1), ("zg", 1, 0),
-    ("s2t", 0, 2), ("zg", 0, 2), ("s2t", 0, 1), ("b2t", 1), ("s1", 1, 0), ("weights",), ("g", 0, 0),
-    ("zg", 0, 3), ("zg", 0, 0), ("part", 0, 0), ("z2t", 1, 2, 1), ("z2t", 1, 2, 0), ("z1", 1, 1), ("s2t", 0, 3),
-    ("r1", 0, 0), ("g", 0, 1), ("part", 0, 1), ("r1", 0, 1), ("z1", 1, 3), ("s2t", 1, 0), ("g", 0, 2),
-    ("part", 0, 2), ("zg", 1, 2), ("g2t", 1, 1), ("g2t", 1, 0), ("r2t", 0, 0), ("s1", 1, 2), ("g", 0, 3),
-    ("part", 0, 3), ("z2t", 1, 1, 1), ("r2t", 0, 1), ("q1", 0, 1), ("q1", 0, 0), ("r1", 0, 3), ("r1", 0, 2),
-    ("g", 1, 0), ("z2t", 1, 1, 0), ("r", 0, 0), ("s1", 1, 1), ("z2t", 1, 3, 1), ("z2t", 1, 3, 0), ("q1", 0, 3),
-    ("s2t", 1, 2), ("r", 0, 1), ("q1", 0, 2), ("s1", 1, 3), ("q2t", 0, 1, 0), ("r2t", 0, 3), ("q2t", 0, 1, 1),
-    ("r2t", 0, 2), ("zg", 1, 1), ("q2t", 0, 0, 0), ("q2t", 0, 0, 1), ("zg", 1, 3), ("part", 1, 0),
-    ("s2t", 1, 1), ("q2t", 0, 3, 0), ("q2t", 0, 3, 1), ("g", 1, 2), ("part", 1, 2), ("s2t", 1, 3), ("r", 0, 3),
-    ("q", 0, 1), ("q2t", 0, 2, 0), ("r1", 1, 2), ("q2t", 0, 2, 1), ("r1", 1, 0), ("t1", 0), ("r", 0, 2),
-    ("g", 1, 1), ("part", 1, 1), ("r1", 1, 1), ("q", 0, 0), ("g", 1, 3), ("part", 1, 3), ("q1", 1, 2),
-    ("r1", 1, 3), ("r2t", 1, 0), ("q", 0, 3), ("q1", 1, 1), ("r2t", 1, 2), ("q1", 1, 3), ("weight", 0),
-    ("r2t", 1, 1), ("t2t", 0, 1), ("t2t", 0, 0), ("ds", 0, 2), ("q", 0, 2), ("weight", 1), ("r2t", 1, 3),
-    ("v1", 0), ("r", 1, 0), ("r", 1, 2), ("ds", 1, 1), ("r", 1, 1), ("q2t", 1, 3, 1), ("q2t", 1, 3, 0),
-    ("ds", 0, 3), ("q2t", 1, 2, 1), ("q2t", 1, 2, 0), ("r", 1, 3), ("t1", 1), ("v2t", 0), ("ds", 1, 2),
-    ("t", 0), ("q1", 1, 0), ("q", 1, 3), ("ds", 1, 3), ("q2t", 1, 1, 1), ("q2t", 1, 1, 0), ("q", 1, 2),
-    ("v", 0), ("back", 0), ("v1", 1), ("ds", 1, 4), ("t2t", 1, 1), ("t2t", 1, 0), ("ds", 1, 0), ("q", 1, 1),
-    ("v2t", 1), ("q2t", 1, 0, 1), ("ds", 0, 0), ("q2t", 1, 0, 0), ("finish", 0), ("ds", 0, 1), ("store", 1),
-    ("t", 1), ("ds", 0, 4), ("q", 1, 0), ("v", 1), ("back", 1), ("store", 0), ("finish", 1),
+    ("enter",), ("ws", 6), ("make", 0), ("ws", 7), ("make", 1), ("ws", 5), ("ws", 4), ("own", 0), ("z1", 0, 0),
+    ("b1", 0), ("g1", 0), ("s1", 0, 0), ("ws", 9), ("b2t", 0), ("ws", 0), ("ws", 2), ("own", 1), ("z1", 0, 1),
+    ("ws", 8), ("z1", 0, 2), ("z1", 0, 3), ("g2t", 0, 0), ("z2t", 0, 0, 1), ("g2t", 0, 1), ("s1", 0, 1),
+    ("z2t", 0, 1, 0), ("s1", 0, 2), ("s2t", 0, 0), ("z2t", 0, 1, 1), ("z2t", 0, 0, 0), ("b1", 1), ("ws", 3),
+    ("z2t", 0, 2, 1), ("z2t", 0, 2, 0), ("z2t", 0, 3, 0), ("z2t", 0, 3, 1), ("ws", 1), ("g1", 1), ("s2t", 0, 1),
+    ("z1", 1, 0), ("s1", 0, 3), ("b2t", 1), ("zg", 0, 2), ("zg", 0, 3), ("zg", 0, 0), ("g", 0, 0), ("s1", 1, 0),
+    ("zg", 0, 1), ("z1", 1, 2), ("s2t", 0, 2), ("z1", 1, 1), ("weights",), ("part", 0, 0), ("s2t", 0, 3),
+    ("r1", 0, 0), ("z1", 1, 3), ("g2t", 1, 1), ("s1", 1, 2), ("g", 0, 1), ("g2t", 1, 0), ("part", 0, 1),
+    ("s1", 1, 1), ("r1", 0, 1), ("s2t", 1, 0), ("z2t", 1, 0, 1), ("g", 0, 3), ("part", 0, 3), ("r1", 0, 3),
+    ("z2t", 1, 0, 0), ("z2t", 1, 2, 1), ("g", 0, 2), ("z2t", 1, 2, 0), ("z2t", 1, 1, 0), ("z2t", 1, 1, 1),
+    ("part", 0, 2), ("q1", 0, 2), ("z2t", 1, 3, 1), ("s2t", 1, 2), ("z2t", 1, 3, 0), ("q1", 0, 1), ("q1", 0, 3),
+    ("r2t", 0, 3), ("q1", 0, 0), ("s1", 1, 3), ("s2t", 1, 1), ("zg", 1, 0), ("r1", 0, 2), ("q2t", 0, 2, 0),
+    ("r2t", 0, 1), ("r2t", 0, 0), ("zg", 1, 2), ("g", 1, 0), ("g", 1, 2), ("q2t", 0, 2, 1), ("zg", 1, 1),
+    ("r", 0, 3), ("t1", 0), ("zg", 1, 3), ("part", 1, 0), ("s2t", 1, 3), ("r1", 1, 0), ("q2t", 0, 0, 1),
+    ("q2t", 0, 3, 0), ("q2t", 0, 3, 1), ("part", 1, 2), ("r2t", 0, 2), ("q2t", 0, 1, 1), ("r1", 1, 2),
+    ("g", 1, 1), ("q2t", 0, 1, 0), ("part", 1, 1), ("r1", 1, 1), ("g", 1, 3), ("q2t", 0, 0, 0), ("part", 1, 3),
+    ("q1", 1, 2), ("r", 0, 2), ("q", 0, 2), ("q1", 1, 0), ("q1", 1, 1), ("r", 0, 1), ("q1", 1, 3), ("r1", 1, 3),
+    ("r2t", 1, 0), ("weight", 1), ("ds", 1, 4), ("t2t", 0, 1), ("t2t", 0, 0), ("q", 0, 3), ("r2t", 1, 2),
+    ("weight", 0), ("r2t", 1, 3), ("v1", 0), ("q2t", 1, 3, 0), ("q", 0, 0), ("ds", 0, 1), ("r", 0, 0),
+    ("q2t", 1, 3, 1), ("r", 1, 3), ("r2t", 1, 1), ("ds", 1, 3), ("t1", 1), ("q2t", 1, 2, 1), ("q", 0, 1),
+    ("q2t", 1, 2, 0), ("r", 1, 2), ("r", 1, 0), ("q2t", 1, 1, 0), ("q2t", 1, 1, 1), ("v2t", 0),
+    ("q2t", 1, 0, 0), ("ds", 0, 4), ("ds", 1, 1), ("q2t", 1, 0, 1), ("q", 1, 3), ("r", 1, 1), ("ds", 0, 2),
+    ("v", 0), ("t", 0), ("back", 0), ("q", 1, 2), ("t2t", 1, 1), ("t2t", 1, 0), ("v1", 1), ("ds", 1, 2),
+    ("q", 1, 1), ("v2t", 1), ("ds", 0, 0), ("ds", 1, 0), ("q", 1, 0), ("finish", 0), ("ds", 0, 3), ("v", 1),
+    ("t", 1), ("back", 1), ("store", 0), ("store", 1), ("finish", 1),
 )
 
 
@@ -172,19 +173,17 @@
         )
 
     def swap_start(kind, way, box, inbound):
-        def one(by, carry):
+        for by in range(1, group):
             swap_copy(kind, way, by, box, inbound).start()
-            return carry
-
-        lax.fori_loop(1, group, one, 0)
         inbound[kind, mine] = box[kind, mine]
 
     def swap_arrived(kind, way, box, inbound):
-        def one(by, carry):
+        for by in range(1, group):
             swap_copy(kind, way, by, box, inbound).wait_recv()
-            return carry
-
-        lax.fori_loop(1, group, one, 0)
+
+    def swap_sent(kind, way, box, inbound):
+        for by in range(1, group):
+            swap_copy(kind, way, by, box, inbound).wait_send()
 
     def make_slots(kind):
         source = (tokens, out_grad)[kind]
@@ -217,6 +216,7 @@
         if kind == 1:
             slot_in_grad_ref[...] = back
             return
+        swap_sent(0, 1, back_outbox, back_inbox)
         for image in range(images):
             grad = lax.dot_general(back[image * slots:(image + 1) * slots], out_grad[image],
                                    (((1,), (1,)), ((), ())), preferred_element_type=F32)
@@ -483,6 +483,8 @@
             arrived("w", i)
         for load in loads:
             load.wait()
+        for kind in range(2):
+            swap_sent(kind, 0, outbox, inbox)
 
     for i in range(2 * PIECES):
         tasks["ws", i] = lambda i=i: weight_piece(i)
@@ -506,20 +508,17 @@
         tasks["store", kind] = lambda kind=kind: store(kind)
 
     assert sorted(tasks, key=str) == sorted(ORDER, key=str)
-    for name in ORDER:
+    counts, waited = [], 0
+    for at, name in enumerate(ORDER):
         tasks[name]()
+        counts.append(len(sent))
+        while at >= LAG and waited < counts[at - LAG]:
+            sent[waited].wait_send()
+            waited += 1
     assert not flying and len(sent) == COPIES
-
-    for copy in sent:
+    for copy in sent[waited:]:
         copy.wait_send()
-
-    def swapped(by, carry):
-        for kind in range(2):
-            swap_copy(kind, 0, by, outbox, inbox).wait_send()
-            swap_copy(kind, 1, by, back_outbox, back_inbox).wait_send()
-        return carry
-
-    lax.fori_loop(1, group, swapped, 0)
+    swap_sent(1, 1, back_outbox, back_inbox)
     for copy in stores:
         copy.wait()
 

time: 101 us -> 97.5 us (0.965)
  Pallas kernels: 97.1 us -> 93.2 us
    pallas_call x1, Pallas kernels: 94 us -> 90.1 us  [shards(): pl.pallas_call(kernel, out_shape=(shape((images * slots, depth), BF16), s...]
where the time goes in v2:
time: 97.5 us; the launch traced here: 97.3 us
  Pallas kernels  93.2 us (96%)
  local copies, waits for them, and re-layouts  3.46 us (4%)
    pallas_call x1, Pallas kernels, shards(): pl.pallas_call(kernel, out_shape=(shape((images * slots, depth), BF16), s...  90.1 us
    unnamed x6, local copies, waits for them, and re-layouts  3.46 us
    pallas_call x1, Pallas kernels, shards(): pl.pallas_call(last_kernel, out_shape=(shape(tokens.shape, BF16), shape(l...  3.1 us

profile of v2, /device:TPU:1, one launch (start us, length us, event | category | flops | bytes accessed | tf_op | source)
XLA Modules:
  0.0 97.3 jit_solution(16156155053614440555)
XLA Ops:
  0.6 0.0 copy-start
  0.6 1.3 %copy-done = bf16[2,256,1280]{2,1,0:T(8,128)(2,1)S(1)} copy-done((bf16[2,256,1280]{2,1,0:T(8,128)(2,1)S(1)}, bf16[2,256,1280]{2,1,0:T(8,128)(2,1)}, u32[]{:S(2)}) %copy-start) | copy-done | bytes 1310744
  1.9 0.0 copy-start.1
  2.0 1.3 %copy-done.1 = bf16[2,256,1280]{2,1,0:T(8,128)(2,1)S(1)} copy-done((bf16[2,256,1280]{2,1,0:T(8,128)(2,1)S(1)}, bf16[2,256,1280]{2,1,0:T(8,128)(2,1)}, u32[]{:S(2)}) %copy-start.1) | copy-done | bytes 1310744
  3.3 0.0 copy-start.2
  3.3 0.8 copy-done.2
  4.1 90.1 %shard_map.84 = (bf16[64,1280]{1,0:T(8,128)(2,1)S(1)}, f32[2,32,256]{2,1,0:T(8,128)S(1)}, bf16[2,320,1280]{2,1,0:T(8,128)(2,1)S(1)}, bf16[2,320,1280]{2,1,0:T(8,128)(2,1)S(1)}) custom-call(bf16[2,256,1280]{2,1,0:T(8,128)(2,1)S(1)} %copy-done, f32[2,32,256]{2,1,0:T(8,128)S(1)} %bitcast.2, bf16[2,256,1280]{2,1,0:T(8,128)(2,1)S(1)} %copy-done.1, ...), custom_call_target="tpu_custom_call" | custom-call | tf_op jit(solution)/shard_map/pallas_call | solution.py:574
  94.2 3.1 %shard_map.85 = (bf16[2,256,1280]{2,1,0:T(8,128)(2,1)}, f32[2,32,256]{2,1,0:T(8,128)}, bf16[2,320,1280]{2,1,0:T(8,128)(2,1)}, bf16[2,320,1280]{2,1,0:T(8,128)(2,1)}) custom-call(bf16[2,256,1280]{2,1,0:T(8,128)(2,1)S(1)} %copy-done, f32[2,32,256]{2,1,0:T(8,128)S(1)} %bitcast.3, bf16[64,1280]{1,0:T(8,128)(2,1)S(1)} %get-tuple-element.12.slot_in_grad_ref, ...), custom_call_target="tpu_custom_call" | custom-call | tf_op jit(solution)/shard_map/pallas_call | solution.py:618
Async XLA Ops:
  0.6 1.3 %copy-start = (bf16[2,256,1280]{2,1,0:T(8,128)(2,1)S(1)}, bf16[2,256,1280]{2,1,0:T(8,128)(2,1)}, u32[]{:S(2)}) copy-start(bf16[2,256,1280]{2,1,0:T(8,128)(2,1)} %tokens.3) | copy-start | bytes 3932164
  1.9 1.3 %copy-start.1 = (bf16[2,256,1280]{2,1,0:T(8,128)(2,1)S(1)}, bf16[2,256,1280]{2,1,0:T(8,128)(2,1)}, u32[]{:S(2)}) copy-start(bf16[2,256,1280]{2,1,0:T(8,128)(2,1)} %out_grad.1) | copy-start | bytes 3932164
  3.3 0.8 copy-start.2

commit v3 on v2

--- a/solution.py
+++ b/solution.py
@@ -9,6 +9,7 @@
 TILE = 128
 SPLIT = 768
 LAG = 90
+STORE_AT = {("v", 0): 25, ("finish", 0): 14}
 PIECES = 5
 COPIES = 2 * 74 + 4 * PIECES
 MESH = pl.DeviceIdType.MESH
@@ -464,13 +465,22 @@
     outs = (w_in_grad_ref, w_out_grad_ref)
     stores = []
 
+    def start_store(source, target, sem):
+        stores.append(pltpu.make_async_copy(source, target, sem))
+        stores[-1].start()
+
+    def store_own(kind):
+        start_store(weight_grads.at[kind, pl.ds(0, width)], outs[kind].at[own], store_sem.at[kind, PIECES])
+
+    def store_piece(kind, i):
+        arrived("d", kind, i)
+        here = pl.ds(i * piece_rows, piece_rows)
+        start_store(mate_grads.at[kind, here], outs[kind].at[1 - own, here], store_sem.at[kind, i])
+
     def store(kind):
         for i in range(PIECES):
-            arrived("d", kind, i)
-        for i, source in enumerate((weight_grads.at[kind, pl.ds(0, width)], mate_grads.at[kind])):
-            stores.append(pltpu.make_async_copy(
-                source, outs[kind].at[(own, 1 - own)[i]], store_sem.at[kind, i]))
-            stores[-1].start()
+            if ("d", kind, i) in flying:
+                store_piece(kind, i)
 
     @task("enter")
     def _():
@@ -502,7 +512,11 @@
             tasks["part", kind, c] = lambda kind=kind, c=c: (forward, backward)[kind](c)
         tasks["back", kind] = lambda kind=kind: send_back(kind)
         tasks["finish", kind] = lambda kind=kind: finish(kind)
-        tasks["weight", kind] = lambda kind=kind: weight_grad(kind)
+        @task("weight", kind)
+        def _(kind=kind):
+            weight_grad(kind)
+            store_own(kind)
+
         for i in range(PIECES):
             tasks["ds", kind, i] = lambda kind=kind, i=i: grad_piece(kind, i)
         tasks["store", kind] = lambda kind=kind: store(kind)
@@ -512,6 +526,10 @@
     for at, name in enumerate(ORDER):
         tasks[name]()
         counts.append(len(sent))
+        if name in STORE_AT:
+            for piece in ORDER[:at + 1 - STORE_AT[name]]:
+                if piece[0] == "ds" and ("d",) + piece[1:] in flying:
+                    store_piece(*piece[1:])
         while at >= LAG and waited < counts[at - LAG]:
             sent[waited].wait_send()
             waited += 1
@@ -605,7 +623,7 @@
             pltpu.VMEM(kept, BF16),
             pltpu.VMEM(kept, BF16),
             pltpu.SemaphoreType.DMA((2,)),
-            pltpu.SemaphoreType.DMA((2, 2)),
+            pltpu.SemaphoreType.DMA((2, PIECES + 1)),
             pltpu.SemaphoreType.DMA((2, 2, group)),
             pltpu.SemaphoreType.DMA((2, 2, group)),
             pltpu.SemaphoreType.DMA((COPIES,)),

time: 97.5 us -> 98 us (level)
  no operation moved by 1% of the time
where the time goes in v3:
time: 98 us; the launch traced here: 97.8 us
  Pallas kernels  93.7 us (96%)
  local copies, waits for them, and re-layouts  3.46 us (4%)
    pallas_call x1, Pallas kernels, shards(): pl.pallas_call(kernel, out_shape=(shape((images * slots, depth), BF16), s...  90.6 us
    unnamed x6, local copies, waits for them, and re-layouts  3.46 us
    pallas_call x1, Pallas kernels, shards(): pl.pallas_call(last_kernel, out_shape=(shape(tokens.shape, BF16), shape(l...  3.11 us

profile of v3, /device:TPU:1, one launch (start us, length us, event | category | flops | bytes accessed | tf_op | source)
XLA Modules:
  0.0 97.8 jit_solution(6947043634359648717)
XLA Ops:
  0.6 0.0 copy-start
  0.6 1.3 %copy-done = bf16[2,256,1280]{2,1,0:T(8,128)(2,1)S(1)} copy-done((bf16[2,256,1280]{2,1,0:T(8,128)(2,1)S(1)}, bf16[2,256,1280]{2,1,0:T(8,128)(2,1)}, u32[]{:S(2)}) %copy-start) | copy-done | bytes 1310744
  1.9 0.0 copy-start.1
  2.0 1.3 %copy-done.1 = bf16[2,256,1280]{2,1,0:T(8,128)(2,1)S(1)} copy-done((bf16[2,256,1280]{2,1,0:T(8,128)(2,1)S(1)}, bf16[2,256,1280]{2,1,0:T(8,128)(2,1)}, u32[]{:S(2)}) %copy-start.1) | copy-done | bytes 1310744
  3.3 0.0 copy-start.2
  3.3 0.8 copy-done.2
  4.1 90.6 %shard_map.84 = (bf16[64,1280]{1,0:T(8,128)(2,1)S(1)}, f32[2,32,256]{2,1,0:T(8,128)S(1)}, bf16[2,320,1280]{2,1,0:T(8,128)(2,1)S(1)}, bf16[2,320,1280]{2,1,0:T(8,128)(2,1)S(1)}) custom-call(bf16[2,256,1280]{2,1,0:T(8,128)(2,1)S(1)} %copy-done, f32[2,32,256]{2,1,0:T(8,128)S(1)} %bitcast.2, bf16[2,256,1280]{2,1,0:T(8,128)(2,1)S(1)} %copy-done.1, ...), custom_call_target="tpu_custom_call" | custom-call | tf_op jit(solution)/shard_map/pallas_call | solution.py:592
  94.7 3.1 %shard_map.85 = (bf16[2,256,1280]{2,1,0:T(8,128)(2,1)}, f32[2,32,256]{2,1,0:T(8,128)}, bf16[2,320,1280]{2,1,0:T(8,128)(2,1)}, bf16[2,320,1280]{2,1,0:T(8,128)(2,1)}) custom-call(bf16[2,256,1280]{2,1,0:T(8,128)(2,1)S(1)} %copy-done, f32[2,32,256]{2,1,0:T(8,128)S(1)} %bitcast.3, bf16[64,1280]{1,0:T(8,128)(2,1)S(1)} %get-tuple-element.12.slot_in_grad_ref, ...), custom_call_target="tpu_custom_call" | custom-call | tf_op jit(solution)/shard_map/pallas_call | solution.py:636
Async XLA Ops:
  0.6 1.3 %copy-start = (bf16[2,256,1280]{2,1,0:T(8,128)(2,1)S(1)}, bf16[2,256,1280]{2,1,0:T(8,128)(2,1)}, u32[]{:S(2)}) copy-start(bf16[2,256,1280]{2,1,0:T(8,128)(2,1)} %tokens.3) | copy-start | bytes 3932164
  1.9 1.3 %copy-start.1 = (bf16[2,256,1280]{2,1,0:T(8,128)(2,1)S(1)}, bf16[2,256,1280]{2,1,0:T(8,128)(2,1)}, u32[]{:S(2)}) copy-start(bf16[2,256,1280]{2,1,0:T(8,128)(2,1)} %out_grad.1) | copy-start | bytes 3932164
  3.3 0.8 copy-start.2

commit v4 on v2

--- a/solution.py
+++ b/solution.py
@@ -173,7 +173,7 @@
         )
 
     def swap_start(kind, way, box, inbound):
-        for by in range(1, group):
+        for by in sorted(range(1, group), key=lambda by: -min(by // 2 % RING, RING - by // 2 % RING)):
             swap_copy(kind, way, by, box, inbound).start()
         inbound[kind, mine] = box[kind, mine]
 

time: 97.5 us -> 97.2 us (level)
  no operation moved by 1% of the time
where the time goes in v4:
time: 97.2 us; the launch traced here: 97 us
  Pallas kernels  92.9 us (96%)
  local copies, waits for them, and re-layouts  3.46 us (4%)
    pallas_call x1, Pallas kernels, shards(): pl.pallas_call(kernel, out_shape=(shape((images * slots, depth), BF16), s...  89.8 us
    unnamed x6, local copies, waits for them, and re-layouts  3.46 us
    pallas_call x1, Pallas kernels, shards(): pl.pallas_call(last_kernel, out_shape=(shape(tokens.shape, BF16), shape(l...  3.11 us

profile of v4, /device:TPU:1, one launch (start us, length us, event | category | flops | bytes accessed | tf_op | source)
XLA Modules:
  0.0 97.0 jit_solution(7017132163940351434)
XLA Ops:
  0.6 0.0 copy-start
  0.6 1.3 %copy-done = bf16[2,256,1280]{2,1,0:T(8,128)(2,1)S(1)} copy-done((bf16[2,256,1280]{2,1,0:T(8,128)(2,1)S(1)}, bf16[2,256,1280]{2,1,0:T(8,128)(2,1)}, u32[]{:S(2)}) %copy-start) | copy-done | bytes 1310744
  1.9 0.0 copy-start.1
  2.0 1.3 %copy-done.1 = bf16[2,256,1280]{2,1,0:T(8,128)(2,1)S(1)} copy-done((bf16[2,256,1280]{2,1,0:T(8,128)(2,1)S(1)}, bf16[2,256,1280]{2,1,0:T(8,128)(2,1)}, u32[]{:S(2)}) %copy-start.1) | copy-done | bytes 1310744
  3.3 0.0 copy-start.2
  3.3 0.8 copy-done.2
  4.1 89.8 %shard_map.84 = (bf16[64,1280]{1,0:T(8,128)(2,1)S(1)}, f32[2,32,256]{2,1,0:T(8,128)S(1)}, bf16[2,320,1280]{2,1,0:T(8,128)(2,1)S(1)}, bf16[2,320,1280]{2,1,0:T(8,128)(2,1)S(1)}) custom-call(bf16[2,256,1280]{2,1,0:T(8,128)(2,1)S(1)} %copy-done, f32[2,32,256]{2,1,0:T(8,128)S(1)} %bitcast.2, bf16[2,256,1280]{2,1,0:T(8,128)(2,1)S(1)} %copy-done.1, ...), custom_call_target="tpu_custom_call" | custom-call | tf_op jit(solution)/shard_map/pallas_call | solution.py:574
  93.9 3.1 %shard_map.85 = (bf16[2,256,1280]{2,1,0:T(8,128)(2,1)}, f32[2,32,256]{2,1,0:T(8,128)}, bf16[2,320,1280]{2,1,0:T(8,128)(2,1)}, bf16[2,320,1280]{2,1,0:T(8,128)(2,1)}) custom-call(bf16[2,256,1280]{2,1,0:T(8,128)(2,1)S(1)} %copy-done, f32[2,32,256]{2,1,0:T(8,128)S(1)} %bitcast.3, bf16[64,1280]{1,0:T(8,128)(2,1)S(1)} %get-tuple-element.12.slot_in_grad_ref, ...), custom_call_target="tpu_custom_call" | custom-call | tf_op jit(solution)/shard_map/pallas_call | solution.py:618
Async XLA Ops:
  0.6 1.3 %copy-start = (bf16[2,256,1280]{2,1,0:T(8,128)(2,1)S(1)}, bf16[2,256,1280]{2,1,0:T(8,128)(2,1)}, u32[]{:S(2)}) copy-start(bf16[2,256,1280]{2,1,0:T(8,128)(2,1)} %tokens.3) | copy-start | bytes 3932164
  1.9 1.3 %copy-start.1 = (bf16[2,256,1280]{2,1,0:T(8,128)(2,1)S(1)}, bf16[2,256,1280]{2,1,0:T(8,128)(2,1)}, u32[]{:S(2)}) copy-start(bf16[2,256,1280]{2,1,0:T(8,128)(2,1)} %out_grad.1) | copy-start | bytes 3932164
  3.3 0.8 copy-start.2
